TPU v7x, 512 devices: a whole 4x8x8 slice. The times are simulated.
512 devices in a mesh: pipe: 8 (over y), seq: 8 (over x, core), dp: 8 (over z).
Axes of the slice: x: 4, y: 8, z: 8, core: 2. Of those that a mesh axis runs over, the one named last changes fastest.
Arguments:
- incoming: bfloat16 [8, 3, 8, 1024, 1536], P('pipe', None, 'dp', 'seq'), may hold values from -9 to 9, as said below
- contacts: int32 [10, 8, 1024], P(None, 'dp', 'seq'), may hold values from 0 to 15
- keyframes: int32 [10, 8, 1024], P(None, 'dp'), may hold values 0 or 1
- timesteps: int32 [10, 8], P(None, 'dp'), may hold values from 0 to 999
- w_query: bfloat16 [8, 1536, 1536], P('pipe', ('seq', 'dp')), may hold values from -1 to 1, as said below
- w_keyval: bfloat16 [8, 1536, 1536], P('pipe', ('seq', 'dp')), may hold values from -1 to 1, as said below
- norm_gain: float32 [8, 1536], P('pipe'), may hold values from 0.5 to 1.5
- time_freq: float32 [8, 1536], P('pipe'), may hold values from 0.0005 to 0.05
- contact_table: bfloat16 [8, 16, 1536], P('pipe'), may hold values from -3 to 3
- key_bias: float32 [8, 16], P('pipe'), may hold values from 0.5 to 4
- attn_gate: float32 [8, 1536], P('pipe'), may hold values from 1 to 4
- head_cotangent: bfloat16 [8, 3, 8, 1024, 256], P('pipe', None, 'dp', 'seq'), may hold values from -6 to 6
Outputs:
- section_out: bfloat16 [8, 3, 8, 1024, 1536], P('pipe', None, 'dp', 'seq')
- head_grad: float32 [8, 1536, 256], P('pipe', ('seq', 'dp'))
Inputs may be any that keep to these rules, and one draw needn't show every extreme that they name: `contacts`: each frame's contact state, four limbs as bits. `incoming`: activations of order one. `w_query`: entries of about 1536 ** -0.5. `w_keyval`: entries of about 1536 ** -0.5.
All inputs are finite; a program needn't handle non-finite values. No bound on the sum of `keyframes` on one device may be relied on, other than what follows from the above.
Results may differ from a plain program's by a relative error of at most 0.014.
Values may be sent and summed in bfloat16 or wider, within the bound.
A program may use at most 64 MiB of HBM per device.

v0:
```python
import jax
import jax.numpy as jnp
from jax import lax
from jax.sharding import PartitionSpec as P

epsilon = 1e-06


def passed_along(value, axis, steps):
    count = lax.axis_size(axis)
    first, last = (max(0, -steps), min(count, count - steps))
    return lax.ppermute(value, axis, [(source, source + steps) for source in range(first, last)])


def body(
    incoming,
    contacts,
    keyframes,
    timesteps,
    w_query,
    w_keyval,
    norm_gain,
    time_freq,
    contact_table,
    key_bias,
    attn_gate,
    head_cotangent,
):
    section_idx = lax.axis_index("pipe")
    seq_idx = lax.axis_index("seq")
    seq_count = lax.axis_size("seq")
    section_count = lax.axis_size("pipe")
    rep_count = lax.axis_size("dp")
    tok_rows = incoming.shape[3]
    width = incoming.shape[4]
    turns = incoming.shape[1]
    frames = tok_rows * seq_count
    heads_all = key_bias.shape[1]
    head_size = width // heads_all
    heads_local = heads_all // seq_count
    kv_width = w_keyval.shape[2]
    kv_local = kv_width // (2 * head_size * seq_count)
    group_size = heads_local // kv_local
    feat_count = head_cotangent.shape[4]
    score_scale = head_size ** (-0.5)
    gathered = (
        lax.all_gather(w_query, ("seq", "dp"), axis=1, tiled=True),
        lax.all_gather(w_keyval, ("seq", "dp"), axis=1, tiled=True),
    )
    wquery = gathered[0][0]
    wkeyval = gathered[1][0]
    gain_row = norm_gain[0]
    freq_row = time_freq[0]
    table = contact_table[0]
    gate_row = attn_gate[0]
    bias_local = lax.dynamic_slice_in_dim(key_bias[0], seq_idx * heads_local, heads_local)
    contact_all = contacts[:, 0, :]
    key_all = keyframes[:, 0, :]
    step_all = timesteps[:, 0]
    labels = jnp.arange(table.shape[0], dtype=jnp.int32)
    outputs = []
    handed = None
    for turn in range(turns):
        fresh_rows = incoming[0, turn, 0]
        if turn == 0:
            current = fresh_rows
        else:
            current = jnp.where(section_idx == 0, fresh_rows, handed)
        batch_idx = turn - section_idx + section_count - 1
        contact_rows = lax.dynamic_index_in_dim(contact_all, batch_idx, 0, keepdims=False)
        key_flags = lax.dynamic_index_in_dim(key_all, batch_idx, 0, keepdims=False).astype(
            jnp.float32
        )
        timestep = lax.dynamic_index_in_dim(step_all, batch_idx, 0, keepdims=False).astype(
            jnp.float32
        )
        onehot = (contact_rows[:, None] == labels[None, :]).astype(jnp.bfloat16)
        embedded = jnp.dot(onehot, table, preferred_element_type=jnp.float32)
        hidden = current.astype(jnp.float32) + embedded
        root_mean = jnp.sqrt(jnp.mean(hidden * hidden, axis=-1, keepdims=True) + epsilon)
        modulation = gain_row * (1.0 + 0.5 * jnp.sin(timestep * freq_row))
        normed = (hidden / root_mean * modulation[None, :]).astype(jnp.bfloat16)
        queries = jnp.dot(normed, wquery, preferred_element_type=jnp.float32).astype(jnp.bfloat16)
        keyval = jnp.dot(normed, wkeyval, preferred_element_type=jnp.float32).astype(jnp.bfloat16)
        query_parts = queries.reshape(tok_rows, seq_count, width // seq_count)
        keyval_parts = keyval.reshape(tok_rows, seq_count, kv_width // seq_count)
        regrouped = (
            lax.all_to_all(query_parts, "seq", split_axis=1, concat_axis=0, tiled=True),
            lax.all_to_all(keyval_parts, "seq", split_axis=1, concat_axis=0, tiled=True),
        )
        query_heads = regrouped[0].reshape(frames, heads_local, head_size)
        keyval_heads = regrouped[1].reshape(frames, kv_local, 2, head_size)
        head_outputs = []
        for head in range(heads_local):
            key_rows = keyval_heads[:, head // group_size, 0]
            value_rows = keyval_heads[:, head // group_size, 1]
            scores = (
                lax.dot_general(
                    query_heads[:, head],
                    key_rows,
                    (((1,), (1,)), ((), ())),
                    preferred_element_type=jnp.float32,
                )
                * score_scale
            )
            scores = scores + bias_local[head] * key_flags[None, :]
            row_max = jnp.max(scores, axis=-1, keepdims=True)
            exponent = jnp.exp(scores - row_max)
            probabilities = (exponent / jnp.sum(exponent, axis=-1, keepdims=True)).astype(
                jnp.bfloat16
            )
            head_outputs.append(
                jnp.dot(probabilities, value_rows, preferred_element_type=jnp.float32).astype(
                    jnp.bfloat16
                )
            )
        attended = jnp.stack(head_outputs, axis=1).reshape(frames, heads_local * head_size)
        returned = lax.all_to_all(attended, "seq", split_axis=0, concat_axis=1, tiled=True)
        output = (hidden + gate_row[None, :] * returned.astype(jnp.float32)).astype(jnp.bfloat16)
        outputs.append(output)
        if turn + 1 < turns:
            handed = passed_along(output, "pipe", 1)
    stacked = jnp.stack(outputs)
    section_out = stacked[None, :, None]
    flat_out = stacked.reshape(turns * tok_rows, width)
    flat_cot = head_cotangent[0, :, 0].reshape(turns * tok_rows, feat_count)
    factor = float(turns * rep_count * frames) ** (-0.5)
    grad_rows = lax.psum_scatter(
        lax.dot_general(
            flat_out, flat_cot, (((0,), (0,)), ((), ())), preferred_element_type=jnp.float32
        )
        * factor,
        ("seq", "dp"),
        scatter_dimension=0,
        tiled=True,
    )
    return (section_out, grad_rows[None])


def solution(mesh):
    in_specs = (
        P("pipe", None, "dp", "seq", None),
        P(None, "dp", "seq"),
        P(None, "dp", None),
        P(None, "dp"),
        P("pipe", ("seq", "dp"), None),
        P("pipe", ("seq", "dp"), None),
        P("pipe", None),
        P("pipe", None),
        P("pipe", None, None),
        P("pipe", None),
        P("pipe", None),
        P("pipe", None, "dp", "seq", None),
    )
    out_specs = (P("pipe", None, "dp", "seq", None), P("pipe", ("seq", "dp"), None))
    return jax.shard_map(body, mesh=mesh, in_specs=in_specs, out_specs=out_specs, check_vma=False)
```

profile of v0, /device:TPU:1, one launch (start us, length us, event | category | flops | bytes accessed | tf_op | source)
XLA Modules:
  0.0 498.7 jit_solution(17415926230523855256)
XLA Ops:
  7.2 0.7 all-gather.3.cloned.1.call-update
  8.0 0.7 all-gather.5.cloned.1.call-update
  8.7 1.4 constant_dynamic-slice_fusion.4
  12.0 0.7 fusion.76
  12.7 1.2 multiply_reduce_fusion.3
  14.0 1.4 multiply_reduce_fusion.2
  15.4 87.5 %all-gather.3.cloned.1.call-done = bf16[1,1536,1536]{2,1,0:T(8,128)(2,1)} async-done(((bf16[1,24,1536]{2,1,0:T(8,128)(2,1)}), bf16[1,1536,1536]{2,1,0:T(8,128)(2,1)}) %all-gather.3.cloned.1.call-update) | async-done | bytes 4718608 | tf_op jit(solution)/shard_map/all_gather | solution.py:47
  102.9 3.2 fusion.24
  106.1 0.9 copy.37
  107.0 3.6 all-to-all-start
  110.6 78.2 %all-gather.5.cloned.1.call-done = bf16[1,1536,1536]{2,1,0:T(8,128)(2,1)} async-done(((bf16[1,24,1536]{2,1,0:T(8,128)(2,1)}), bf16[1,1536,1536]{2,1,0:T(8,128)(2,1)}) %all-gather.5.cloned.1.call-update) | async-done | bytes 4718608 | tf_op jit(solution)/shard_map/all_gather | solution.py:48
  188.8 3.2 fusion.33
  192.0 0.9 copy.39
  192.9 3.6 all-to-all-start.1
  197.2 2.0 convert_multiply_fusion.1
  199.7 4.9 all-to-all-done.1
  205.1 0.8 fusion.12
  205.9 0.9 fusion.18
  206.8 1.2 fusion.54
  207.9 0.8 fusion.13
  208.7 0.9 fusion.19
  209.6 1.2 fusion.55
  211.0 0.8 copy.41
  211.8 4.2 all-to-all-start.2
  216.0 8.1 %all-to-all-done.2 = bf16[8,128,192]{1,2,0:T(8,128)(2,1)S(1)} async-done(((bf16[8,128,192]{1,2,0:T(8,128)(2,1)}), bf16[8,128,192]{1,2,0:T(8,128)(2,1)S(1)}, u32[]{:S(2)}, u32[]{:S(2)}) %all-to-all-start.2) | async-done | bytes 393248 | tf_op jit(solution)/shard_map/all_to_all | solution.py:118
  224.5 3.1 collective-permute-start
  227.7 7.5 %collective-permute-done = bf16[128,1536]{1,0:T(8,128)(2,1)S(1)} collective-permute-done((bf16[128,1536]{1,0:T(8,128)(2,1)S(1)}, bf16[128,1536]{1,0:T(8,128)(2,1)S(1)}, u32[]{:S(2)}, u32[]{:S(2)}) %collective-permute-start) | collective-permute-done | bytes 393248 | tf_op jit(solution)/shard_map/ppermute | solution.py:12
  235.2 1.4 multiply_reduce_fusion.1
  236.6 3.2 fusion.27
  239.8 0.9 copy.43
  240.7 5.1 %all-to-all-start.3 = ((bf16[128,8,192]{0,2,1:T(8,128)(2,1)}), bf16[128,8,192]{0,2,1:T(8,128)(2,1)S(1)}, u32[]{:S(2)}, u32[]{:S(2)}) async-start(bf16[128,8,192]{0,2,1:T(8,128)(2,1)} %bitcast.28), calls=%async_computation.3 | async-start | bytes 786432 | tf_op jit(solution)/shard_map/all_to_all | solution.py:88
  245.8 3.2 fusion.36
  249.0 0.9 copy.45
  249.9 4.0 all-to-all-done.3
  253.9 4.2 all-to-all-start.4
  258.6 7.7 %all-to-all-done.4 = bf16[128,8,192]{0,2,1:T(8,128)(2,1)S(1)} async-done(((bf16[128,8,192]{0,2,1:T(8,128)(2,1)}), bf16[128,8,192]{0,2,1:T(8,128)(2,1)S(1)}, u32[]{:S(2)}, u32[]{:S(2)}) %all-to-all-start.4) | async-done | bytes 393248 | tf_op jit(solution)/shard_map/all_to_all | solution.py:89
  266.7 0.8 fusion.14
  267.5 0.9 fusion.20
  268.4 1.2 fusion.56
  269.6 0.8 fusion.15
  270.4 0.9 fusion.21
  271.3 1.2 fusion.57
  272.6 11.3 %all_to_all.129 = bf16[8,128,192]{1,2,0:T(8,128)(2,1)S(1)} all-to-all(bf16[8,128,192]{1,2,0:T(8,128)(2,1)S(1)} %copy.47), channel_id=1, replica_groups=mesh['pipe'=8,'seq'=8,'dp'=8] {'seq'}, dimensions={0} | all-to-all | bytes 786432 | tf_op jit(solution)/shard_map/all_to_all | solution.py:118
  284.4 4.1 collective-permute-start.1
  288.9 7.2 %collective-permute-done.1 = bf16[128,1536]{1,0:T(8,128)(2,1)S(1)} collective-permute-done((bf16[128,1536]{1,0:T(8,128)(2,1)S(1)}, bf16[128,1536]{1,0:T(8,128)(2,1)S(1)}, u32[]{:S(2)}, u32[]{:S(2)}) %collective-permute-start.1) | collective-permute-done | bytes 393248 | tf_op jit(solution)/shard_map/ppermute | solution.py:12
  296.1 1.2 multiply_reduce_fusion
  297.3 3.2 fusion.30
  300.5 0.9 copy.49
  301.4 5.1 %all-to-all-start.6 = ((bf16[128,8,192]{0,2,1:T(8,128)(2,1)}), bf16[128,8,192]{0,2,1:T(8,128)(2,1)S(1)}, u32[]{:S(2)}, u32[]{:S(2)}) async-start(bf16[128,8,192]{0,2,1:T(8,128)(2,1)} %bitcast.48), calls=%async_computation.6 | async-start | bytes 786432 | tf_op jit(solution)/shard_map/all_to_all | solution.py:88
  306.6 3.2 fusion.39
  309.7 0.9 copy.51
  310.6 4.0 all-to-all-done.6
  314.6 4.2 all-to-all-start.7
  319.3 7.7 %all-to-all-done.7 = bf16[128,8,192]{0,2,1:T(8,128)(2,1)S(1)} async-done(((bf16[128,8,192]{0,2,1:T(8,128)(2,1)}), bf16[128,8,192]{0,2,1:T(8,128)(2,1)S(1)}, u32[]{:S(2)}, u32[]{:S(2)}) %all-to-all-start.7) | async-done | bytes 393248 | tf_op jit(solution)/shard_map/all_to_all | solution.py:89
  327.4 0.8 fusion.16
  328.2 0.9 fusion.22
  329.1 1.2 fusion.58
  330.3 0.8 fusion.17
  331.1 0.9 fusion.23
  332.0 1.2 fusion.59
  333.3 11.3 %all_to_all.130 = bf16[8,128,192]{1,2,0:T(8,128)(2,1)S(1)} all-to-all(bf16[8,128,192]{1,2,0:T(8,128)(2,1)S(1)} %copy.53), channel_id=1, replica_groups=mesh['pipe'=8,'seq'=8,'dp'=8] {'seq'}, dimensions={0} | all-to-all | bytes 786432 | tf_op jit(solution)/shard_map/all_to_all | solution.py:118
  345.1 1.2 pad_maximum_fusion
  346.3 1.8 convolution_multiply_fusion
  348.1 144.1 %reduce-scatter.4.cloned.1.call-done = f32[24,256]{1,0:T(8,128)} async-done(((f32[1536,256]{1,0:T(8,128)}), f32[24,256]{1,0:T(8,128)}) %reduce-scatter.4.cloned.1.call-update) | async-done | bytes 24592
  (49 shorter events, 5.4 us)
Async XLA Ops:
  7.2 339.1 %copy-start = (bf16[1,3,1,128,256]{4,3,2,1,0:T(8,128)(2,1)S(1)}, bf16[1,3,1,128,256]{4,3,2,1,0:T(8,128)(2,1)}, u32[]{:S(2)}) copy-start(bf16[1,3,1,128,256]{4,3,2,1,0:T(8,128)(2,1)} %param.23) | copy-start | bytes 589828
  7.2 95.7 %all-gather.3.cloned.1.call-start = ((), (), s32[]{:S(2)}) async-start(), calls=%async_computation.10 | async-start | bytes 4792320 | tf_op jit(solution)/shard_map/all_gather | solution.py:47
  7.9 180.9 %all-gather.5.cloned.1.call-start = ((), (), s32[]{:S(2)}) async-start(), calls=%async_computation.11 | async-start | bytes 4792320 | tf_op jit(solution)/shard_map/all_gather | solution.py:48
  107.0 85.9 %all-to-all-start = ((bf16[128,8,192]{0,2,1:T(8,128)(2,1)}), bf16[128,8,192]{0,2,1:T(8,128)(2,1)S(1)}, u32[]{:S(2)}, u32[]{:S(2)}) async-start(bf16[128,8,192]{0,2,1:T(8,128)(2,1)} %bitcast.5), calls=%async_computation | async-start | bytes 786432 | tf_op jit(solution)/shard_map/all_to_all | solution.py:88
  110.6 85.9 %copy-start.3 = (f32[1,16]{1,0:T(1,128)S(1)}, f32[1,16]{1,0:T(1,128)}, u32[]{:S(2)}) copy-start(f32[1,16]{1,0:T(1,128)} %param.21) | copy-start | bytes 196
  192.9 11.7 %all-to-all-start.1 = ((bf16[128,8,192]{0,2,1:T(8,128)(2,1)}), bf16[128,8,192]{0,2,1:T(8,128)(2,1)S(1)}, u32[]{:S(2)}, u32[]{:S(2)}) async-start(bf16[128,8,192]{0,2,1:T(8,128)(2,1)} %bitcast.10), calls=%async_computation.1 | async-start | bytes 786432 | tf_op jit(solution)/shard_map/all_to_all | solution.py:89
  209.6 6.4 %copy-start.2 = (f32[1,1536]{1,0:T(1,128)S(1)}, f32[1,1536]{1,0:T(1,128)}, u32[]{:S(2)}) copy-start(f32[1,1536]{1,0:T(1,128)} %param.22) | copy-start | bytes 18436
  210.8 24.4 %copy-start.1 = (bf16[1,16,1536]{2,1,0:T(8,128)(2,1)S(1)}, bf16[1,16,1536]{2,1,0:T(8,128)(2,1)}, u32[]{:S(2)}) copy-start(bf16[1,16,1536]{2,1,0:T(8,128)(2,1)} %param.20) | copy-start | bytes 147460
  211.8 12.3 %all-to-all-start.2 = ((bf16[8,128,192]{1,2,0:T(8,128)(2,1)}), bf16[8,128,192]{1,2,0:T(8,128)(2,1)S(1)}, u32[]{:S(2)}, u32[]{:S(2)}) async-start(bf16[8,128,192]{1,2,0:T(8,128)(2,1)} %copy.41), calls=%async_computation.2 | async-start | bytes 786432 | tf_op jit(solution)/shard_map/all_to_all | solution.py:118
  224.5 10.7 %collective-permute-start = (bf16[128,1536]{1,0:T(8,128)(2,1)S(1)}, bf16[128,1536]{1,0:T(8,128)(2,1)S(1)}, u32[]{:S(2)}, u32[]{:S(2)}) collective-permute-start(bf16[128,1536]{1,0:T(8,128)(2,1)S(1)} %add_convert_fusion.2), channel_id=1, source_target_pairs={{0,64},{64,128},{128,192},{192,256},{256,320},{320,384},{384,448},... | collective-permute-start | bytes 1179656 | tf_op jit(solution)/shard_map/ppermute | solution.py:12
  240.7 13.2 %all-to-all-start.3 = ((bf16[128,8,192]{0,2,1:T(8,128)(2,1)}), bf16[128,8,192]{0,2,1:T(8,128)(2,1)S(1)}, u32[]{:S(2)}, u32[]{:S(2)}) async-start(bf16[128,8,192]{0,2,1:T(8,128)(2,1)} %bitcast.28), calls=%async_computation.3 | async-start | bytes 786432 | tf_op jit(solution)/shard_map/all_to_all | solution.py:88
  253.9 12.3 %all-to-all-start.4 = ((bf16[128,8,192]{0,2,1:T(8,128)(2,1)}), bf16[128,8,192]{0,2,1:T(8,128)(2,1)S(1)}, u32[]{:S(2)}, u32[]{:S(2)}) async-start(bf16[128,8,192]{0,2,1:T(8,128)(2,1)} %bitcast.32), calls=%async_computation.4 | async-start | bytes 786432 | tf_op jit(solution)/shard_map/all_to_all | solution.py:89
  284.4 11.7 %collective-permute-start.1 = (bf16[128,1536]{1,0:T(8,128)(2,1)S(1)}, bf16[128,1536]{1,0:T(8,128)(2,1)S(1)}, u32[]{:S(2)}, u32[]{:S(2)}) collective-permute-start(bf16[128,1536]{1,0:T(8,128)(2,1)S(1)} %add_convert_fusion.1), channel_id=1, source_target_pairs={{0,64},{64,128},{128,192},{192,256},{256,320},{320,384},{384,448},... | collective-permute-start | bytes 1179656 | tf_op jit(solution)/shard_map/ppermute | solution.py:12
  301.4 13.2 %all-to-all-start.6 = ((bf16[128,8,192]{0,2,1:T(8,128)(2,1)}), bf16[128,8,192]{0,2,1:T(8,128)(2,1)S(1)}, u32[]{:S(2)}, u32[]{:S(2)}) async-start(bf16[128,8,192]{0,2,1:T(8,128)(2,1)} %bitcast.48), calls=%async_computation.6 | async-start | bytes 786432 | tf_op jit(solution)/shard_map/all_to_all | solution.py:88
  314.6 12.3 %all-to-all-start.7 = ((bf16[128,8,192]{0,2,1:T(8,128)(2,1)}), bf16[128,8,192]{0,2,1:T(8,128)(2,1)S(1)}, u32[]{:S(2)}, u32[]{:S(2)}) async-start(bf16[128,8,192]{0,2,1:T(8,128)(2,1)} %bitcast.52), calls=%async_computation.7 | async-start | bytes 786432 | tf_op jit(solution)/shard_map/all_to_all | solution.py:89
  318.9 173.3 %reduce-scatter.4.cloned.1.call-start = ((), (), s32[]{:S(2)}) async-start(), calls=%async_computation.12 | async-start | bytes 1597440
Sparse Core Ops, SparseCore 0:
  11.3 91.5 all-gather.2
  106.2 82.5 all-gather.4
  348.2 143.9 reduce-scatter.3
where the time goes:
time: 504 us; the launch traced here: 499 us
  waiting for transfers between devices  362 us (72%)
  starting transfers between devices  37.5 us (7%)
  matrix products  35.7 us (7%)
  blocking collectives  22.7 us (5%)
  between operations  16.1 us (3%)
  local copies, waits for them, and re-layouts  12.8 us (3%)
  other arithmetic  11.6 us (2%)
    unnamed x4, waiting for transfers between devices  145 us
    all_gather x1, waiting for transfers between devices, body(): lax.all_gather(w_query, ('seq', 'dp'), axis=1, tiled=True)  87.5 us
    all_gather x1, waiting for transfers between devices, body(): lax.all_gather(w_keyval, ('seq', 'dp'), axis=1, tiled=True)  78.2 us
    all_to_all x2, blocking collectives, body(): lax.all_to_all(attended, 'seq', split_axis=0, concat_axis=1, tiled=True)  22.7 us
    all_to_all x3, waiting for transfers between devices, body(): lax.all_to_all(keyval_parts, 'seq', split_axis=1, concat_axis=0, tiled=True)  20.2 us
    ppermute x2, waiting for transfers between devices, passed_along(): lax.ppermute(value, axis, [(source, source + steps) for source in range(f...  14.7 us
    all_to_all x3, starting transfers between devices, body(): lax.all_to_all(query_parts, 'seq', split_axis=1, concat_axis=0, tiled=True)  13.8 us
    all_to_all x3, starting transfers between devices, body(): lax.all_to_all(keyval_parts, 'seq', split_axis=1, concat_axis=0, tiled=True)  12.1 us
  transfers between devices with their start and end apart: 12, of which 11 were waited for; matrix products, arithmetic and copies ran while one was open for 5% of the time, Pallas kernels for 0%

commit v1 on v0

v1 whole, which is shorter than its diff:
```python
import functools
import math

import jax
import jax.numpy as jnp
from jax import lax
from jax.experimental import pallas as pl
from jax.experimental.pallas import tpu as pltpu
from jax.sharding import PartitionSpec as P

BF16 = jnp.bfloat16
F32 = jnp.float32
MESH = pl.DeviceIdType.MESH
EPSILON = 1e-06
LOG2E = math.log2(math.e)
XN = 4
ZN = 8
SN = 8
TURNS = 3
D = 1536
CW = 384
HEAD = 96
B = 128


def dot(a, b):
    return jnp.dot(a, b, preferred_element_type=F32)


def dot_t(a, b):
    return lax.dot_general(a, b, (((0,), (0,)), ((), ())), preferred_element_type=F32)


def dot_nt(a, b):
    return lax.dot_general(a, b, (((1,), (1,)), ((), ())), preferred_element_type=F32)


def kernel(
    inc, contacts, keyframes, timesteps, wq, wkv, gain, freq, table, kbias, gate, cot,
    out, grad,
    xg, wr, wp, ctv, cotv, stg, rcv, act, asend, arecv, atto, ob, modv, psel, pw, qpad, gacc, grec, gsum, grz,
    xs, xrv, lx, ys, yr, ws, wrv, wl, zs, zr, bs, br, cs, cr, ks, kr, qs, qr, asm, arm, osm, orm, gs, gr,
):
    s = lax.axis_index("pipe")
    i = lax.axis_index("seq")
    j = lax.axis_index("dp")
    x = lax.div(i, 2)
    c = lax.rem(i, 2)
    first = lax.div(SN - s, SN)

    def xat(d):
        return lax.rem(x + d + XN, XN)

    def zat(d):
        return lax.rem(j + d + ZN, ZN)

    def xdev(d):
        return (s, 2 * xat(d) + c, j)

    def zdev(d):
        return (s, i, zat(d))

    sib = (s, 2 * x + 1 - c, j)
    ynext = (lax.rem(s + 1, SN), i, j)
    yprev = (lax.rem(s + SN - 1, SN), i, j)

    def remote(src, dst, send, recv, device):
        return pltpu.make_async_remote_copy(
            src_ref=src, dst_ref=dst, send_sem=send, recv_sem=recv, device_id=device, device_id_type=MESH
        )

    def cols(b):
        return pl.ds(pl.multiple_of(b * CW, 128), CW)

    def rows(r):
        return pl.ds(pl.multiple_of(r * B, B), B)

    barrier = pltpu.get_barrier_semaphore()
    peers = [xdev(1), xdev(2), xdev(3), sib, ynext, yprev] + [zdev(d) for d in range(1, ZN)]
    for peer in peers:
        pl.semaphore_signal(barrier, inc=1, device_id=peer, device_id_type=MESH)

    own_x0 = pltpu.make_async_copy(inc.at[0, 0, 0], xg.at[0, rows(x)], lx.at[0])
    own_x0.start()
    own_ct = pltpu.make_async_copy(contacts, ctv.at[x], cs.at[0])
    own_ct.start()
    own_cot = pltpu.make_async_copy(cot.at[0, :, 0], cotv.at[x], lx.at[3])
    own_cot.start()
    own_w = [
        pltpu.make_async_copy(w.at[0, :, cols(x)], wr.at[c, j, x, :, CW * n : CW * n + CW], wl.at[n])
        for n, w in enumerate((wq, wkv))
    ]
    for copy in own_w:
        copy.start()

    def own_later(t):
        return pltpu.make_async_copy(inc.at[0, t, 0], xg.at[t, rows(x)], lx.at[t])

    @pl.when(s == 0)
    def _():
        own_later(1).start()
        own_later(2).start()

    pl.semaphore_wait(barrier, len(peers))

    def w_piece(d, n, w):
        return remote(
            w.at[0, :, cols(xat(d))],
            wr.at[c, j, x, :, CW * n : CW * n + CW],
            ws.at[d - 1, n],
            wrv.at[d - 1, n],
            xdev(d),
        )

    def w_arrival(d, n):
        here = wr.at[c, j, xat(-d), :, CW * n : CW * n + CW]
        return remote(here, here, ws.at[d - 1, n], wrv.at[d - 1, n], xdev(d))

    for d in (1, 3, 2):
        for n, w in enumerate((wq, wkv)):
            w_piece(d, n, w).start()

    def ct_piece(d, src):
        return remote(ctv.at[src], ctv.at[src], cs.at[d], cr.at[d], xdev(d))

    def cot_piece(t, d, src):
        return remote(cotv.at[src, t], cotv.at[src, t], ks.at[t, d - 1], kr.at[t, d - 1], xdev(d))

    def piece(t, a, b):
        if t == 0:
            r, n = b, a
        else:
            r, n = a + first * (b - a), b + first * (a - b)
        return xg.at[t, rows(r), cols(n)]

    def x_send(t, a, way):
        dst = piece(t, a, x)
        src = inc.at[0, 0, 0, :, CW * a : CW * a + CW] if t == 0 else dst
        return remote(src, dst, xs.at[t, a, way], xrv.at[t, a, way], xdev(1 - 2 * way))

    def x_arrival(t, a, way):
        here = piece(t, a, xat(2 * way - 1))
        return remote(here, here, xs.at[t, a, way], xrv.at[t, a, way], xdev(1))

    def x_pass(t, a):
        way = a % 2
        here = piece(t, a, xat(2 * way - 1))
        return remote(here, here, xs.at[t, a, 2], xrv.at[t, a, 2], xdev(1 - 2 * way))

    def x_passed(t, a):
        here = piece(t, a, xat(2))
        return remote(here, here, xs.at[t, a, 2], xrv.at[t, a, 2], xdev(1))

    def y_copy(t, r):
        return remote(ob.at[t, r], xg.at[t + 1, rows(r), cols(x)], ys.at[t, r], yr.at[t, r], ynext)

    def x_start(t, a):
        if t > 0:
            @pl.when(s > 0)
            def _():
                y_copy(t - 1, a).wait_recv()

            if a == 0:
                @pl.when(s == 0)
                def _():
                    own_later(t).wait()

        x_send(t, a, 0).start()
        x_send(t, a, 1).start()

    def x_forward(t, a):
        x_arrival(t, a, a % 2).wait_recv()
        x_pass(t, a).start()

    def x_finish(t, a):
        x_arrival(t, a, 1 - a % 2).wait_recv()
        x_passed(t, a).wait_recv()

    for a in range(XN):
        x_start(0, a)
    own_ct.wait()
    for d in (1, 2, 3):
        ct_piece(d, x).start()

    lane = lax.broadcasted_iota(jnp.int32, (1, 128), 1)
    head_lane = lax.broadcasted_iota(jnp.int32, (1, 16), 1)
    for h in range(4):
        b = jnp.sum(jnp.where(head_lane == 4 * x + h, kbias[...], 0.0), axis=1, keepdims=True) * LOG2E
        high = b.astype(BF16).astype(F32)
        qpad[h : h + 1, :] = jnp.where(lane == HEAD, high, 0.0) + jnp.where(lane == HEAD + 1, b - high, 0.0)
    for t in range(TURNS):
        step = timesteps[t - s + SN - 1, 0].astype(F32)
        modv[t : t + 1, :] = gain[...] * (1.0 + 0.5 * jnp.sin(step * freq[...]))
    row = lax.broadcasted_iota(jnp.int32, (512, CW), 0)
    col = lax.broadcasted_iota(jnp.int32, (512, CW), 1)
    slot = lax.shift_right_logical(row, 7)
    low = row - slot * 128
    head = jnp.where(slot < 2, slot + 2 * c, slot - 2 * c)
    psel[...] = jnp.where((low < HEAD) & (col == head * HEAD + low), 1.0, 0.0).astype(BF16)
    row = lax.broadcasted_iota(jnp.int32, (CW, 512), 0)
    col = lax.broadcasted_iota(jnp.int32, (CW, 512), 1)
    slot = lax.shift_right_logical(col, 7)
    low = col - slot * 128
    pw[...] = jnp.where((low < HEAD) & (row == slot * HEAD + low), 1.0, 0.0).astype(BF16)

    def z_blocks(k, way):
        block = zat(-k) if way == 0 else zat(k)
        part = wr.at[c, block] if k < ZN // 2 else wr.at[c, block, pl.ds(2 * way, 2)]
        return part

    def z_send(k, way):
        block = zat(1 - k) if way == 0 else zat(k - 1)
        part = wr.at[c, block] if k < ZN // 2 else wr.at[c, block, pl.ds(2 * way, 2)]
        return remote(part, part, zs.at[k - 1, way], zr.at[k - 1, way], zdev(1 - 2 * way))

    def z_arrival(k, way):
        part = z_blocks(k, way)
        return remote(part, part, zs.at[k - 1, way], zr.at[k - 1, way], zdev(1))

    def sib_part(core, k, way):
        block = zat(-k) if way == 0 else zat(k)
        return wr.at[core, block] if k < ZN // 2 else wr.at[core, block, pl.ds(2 * way, 2)]

    def sib_send(core, k, way):
        part = sib_part(core, k, way)
        return remote(part, part, bs.at[k, way], br.at[k, way], sib)

    for copy in own_w:
        copy.wait()
    for d in (1, 3, 2):
        for n in range(2):
            w_arrival(d, n).wait_recv()
    z_send(1, 0).start()
    z_send(1, 1).start()
    sib_send(c, 0, 0).start()
    x_forward(0, 0)
    x_forward(0, 1)

    def z_step(k):
        for way in range(2):
            z_arrival(k, way).wait_recv()
            if k < ZN // 2:
                z_send(k + 1, way).start()
            sib_send(c, k, way).start()

    z_step(1)
    x_forward(0, 2)
    x_forward(0, 3)
    for k in range(2, ZN // 2 + 1):
        z_step(k)
    own_x0.wait()
    for a in range(XN):
        x_finish(0, a)
    for d in (1, 2, 3):
        ct_piece(d, xat(-d)).wait_recv()
    sib_send(1 - c, 0, 0).wait_recv()
    for k in range(1, ZN // 2 + 1):
        for way in range(2):
            sib_send(1 - c, k, way).wait_recv()

    def prepare(n, _):
        cc, xx = lax.rem(n, 2), lax.div(n, 2)
        block = wr[cc, :, xx].astype(F32).reshape(ZN * 24, 2 * CW).astype(BF16)
        dst = pl.ds(pl.multiple_of(n * 192, 64), 192)
        wp[dst, 0:512] = dot(block[:, :CW], pw[...]).astype(BF16)
        wp[dst, 512:1024] = dot(block[:, CW:], pw[...]).astype(BF16)
        return 0

    lax.fori_loop(0, 2 * XN, prepare, 0)

    def contact_rows(t, r):
        return ctv[r, t - s + SN - 1]

    def onehot(values):
        count = values.shape[1]
        states = lax.broadcasted_iota(jnp.int32, (16, count), 0)
        return jnp.where(states == values, 1.0, 0.0).astype(BF16)

    place = lax.broadcasted_iota(jnp.int32, (16, 128), 0)
    place_lane = lax.broadcasted_iota(jnp.int32, (16, 128), 1)
    flag_lanes = jnp.where(
        (place == 0) & ((place_lane == HEAD) | (place_lane == HEAD + 1)), 1.0, 0.0
    ).astype(BF16)
    ones_lane = jnp.where(lane == HEAD, 1.0, 0.0)

    def q_exchange(t, p):
        span = pl.ds(256 * p, 256)
        return remote(stg.at[t, 1 - c, :, span], rcv.at[t, :, span], qs.at[t, p], qr.at[t, p], sib)

    def project(t, p):
        turn = t - s + SN - 1
        span = slice(256 * p, 256 * p + 256)
        flags = []
        scales = []
        for q in range(2):
            r = 2 * p + q
            inner = slice(B * r, B * r + B)
            hidden = xg[t, inner, :].astype(F32) + dot_t(onehot(contact_rows(t, r)), table[0])
            square = jnp.sum(hidden * hidden, axis=1, keepdims=True)
            act[inner, :] = (hidden * modv[t : t + 1, :]).astype(BF16)
            scales.append(lax.rsqrt(square * (1.0 / D) + EPSILON))
            flag = keyframes[turn, :, pl.ds(pl.multiple_of((2 * r + c) * B, B), B)]
            flag = jnp.where(place == 0, flag.astype(F32), 0.0).astype(BF16)
            flags.append(dot_t(flag, flag_lanes))
        scale = jnp.concatenate(scales, axis=0)
        flag = jnp.concatenate(flags, axis=0)
        result = dot(act[span, :], wp[...])
        scale_q = scale * (LOG2E * HEAD ** (-0.5))
        for h in range(4):
            stg[t, h // 2, h % 2, span, :] = (
                result[:, 128 * h : 128 * h + 128] * scale_q + qpad[h : h + 1, :]
            ).astype(BF16)
        for h in range(2):
            at = 512 + 256 * h
            stg[t, h, 2, span, :] = (result[:, at : at + 128] * scale + flag).astype(BF16)
            stg[t, h, 3, span, :] = (result[:, at + 128 : at + 256] * scale + ones_lane).astype(BF16)
        q_exchange(t, p).start()

    def a_exchange(t, r):
        return remote(asend.at[t, r], arecv.at[t, r], asm.at[t, r], arm.at[t, r], sib)

    def attend(t, r):
        for h in range(2):
            q = jnp.concatenate([stg[t, c, h, rows(r), :], rcv[t, h, rows(r), :]], axis=0)
            s0 = dot_nt(q, stg[t, c, 2])
            s1 = dot_nt(q, rcv[t, 2])
            top = jnp.maximum(jnp.max(s0, axis=1, keepdims=True), jnp.max(s1, axis=1, keepdims=True))
            total = dot(jnp.exp2(s0 - top).astype(BF16), stg[t, c, 3])
            total = total + dot(jnp.exp2(s1 - top).astype(BF16), rcv[t, 3])
            result = (total * (1.0 / total[:, HEAD : HEAD + 1])).astype(BF16)
            atto[r, h] = result[:B]
            asend[t, r, h] = result[B:]
        a_exchange(t, r).start()

    def finish(t, r):
        a_exchange(t, r).wait_recv()
        heads = jnp.concatenate([atto[r, 0], atto[r, 1], arecv[t, r, 0], arecv[t, r, 1]], axis=1)
        attended = dot(heads, psel[...])
        hidden = xg[t, rows(r), cols(x)].astype(F32) + dot_t(
            onehot(contact_rows(t, r)), table[0, :, cols(x)]
        )
        ob[t, r] = (hidden + gate[:, cols(x)] * attended).astype(BF16)
        if t + 1 < TURNS:
            @pl.when(s < SN - 1)
            def _():
                y_copy(t, r).start()

    def out_copy(t, d):
        return remote(
            ob.at[t, xat(d)], out.at[0, t, 0, :, cols(x)], osm.at[t, d], orm.at[t, d], xdev(d)
        )

    def out_arrival(t, d):
        return remote(
            ob.at[t, xat(d)], out.at[0, t, 0, :, cols(xat(-d))], osm.at[t, d], orm.at[t, d], xdev(d)
        )

    def out_own(t):
        return pltpu.make_async_copy(ob.at[t, x], out.at[0, t, 0, :, cols(x)], osm.at[t, 0])

    for t in range(TURNS):
        if t > 0:
            x_forward(t, 0)
            x_forward(t, 1)
            x_start(t, 2)
            x_start(t, 3)
            x_forward(t, 2)
            x_forward(t, 3)
            for a in range(XN):
                x_finish(t, a)
        project(t, 0)
        project(t, 1)
        if t == 0:
            own_cot.wait()
        for d in (1, 2, 3):
            cot_piece(t, d, x).start()
        if t > 0:
            out_own(t - 1).start()
            for d in (1, 2, 3):
                out_copy(t - 1, d).start()
        q_exchange(t, 0).wait_recv()
        q_exchange(t, 1).wait_recv()

        def step(r, _, t=t):
            attend(t, r)

            @pl.when(r > 0)
            def _():
                finish(t, r - 1)

            return 0

        lax.fori_loop(0, XN, step, 0)
        if t + 1 < TURNS:
            x_start(t + 1, 0)
        finish(t, XN - 1)
        if t + 1 < TURNS:
            x_start(t + 1, 1)
        else:
            out_own(t).start()
            for d in (1, 2, 3):
                out_copy(t, d).start()
        for d in (1, 2, 3):
            cot_piece(t, d, xat(-d)).wait_recv()
        share = dot_t(ob[t].reshape(XN * B, CW), cotv[:, t].reshape(XN * B, 256))
        gacc[...] = share if t == 0 else gacc[...] + share

    g_sib = remote(
        gacc.at[pl.ds(pl.multiple_of((1 - c) * 192, 64), 192)], grec, gs.at[0], gr.at[0], sib
    )
    g_sib.start()
    g_sib.wait_recv()
    gsum[...] = gacc[pl.ds(pl.multiple_of(c * 192, 64), 192), :] + grec[...]

    def g_copy(d):
        return remote(
            gsum.at[pl.ds(pl.multiple_of(24 * zat(d), 8), 24)], grz.at[d - 1], gs.at[d], gr.at[d], zdev(d)
        )

    for d in (4, 3, 5, 2, 6, 1, 7):
        g_copy(d).start()
    total = gsum[pl.ds(pl.multiple_of(24 * j, 8), 24), :]
    for d in (1, 7, 2, 6, 3, 5, 4):
        g_copy(d).wait_recv()
        total = total + grz[d - 1]
    grad[0] = total * (float(TURNS * ZN * 1024) ** (-0.5))

    for d in (1, 2, 3):
        for n, w in enumerate((wq, wkv)):
            w_piece(d, n, w).wait_send()
        ct_piece(d, x).wait_send()
    for k in range(ZN // 2 + 1):
        for way in range(2):
            if k > 0:
                z_send(k, way).wait_send()
            if k > 0 or way == 0:
                sib_send(c, k, way).wait_send()
    for t in range(TURNS):
        out_own(t).wait()
        for d in (1, 2, 3):
            cot_piece(t, d, x).wait_send()
            out_copy(t, d).wait_send()
            out_arrival(t, d).wait_recv()
        for a in range(XN):
            x_send(t, a, 0).wait_send()
            x_send(t, a, 1).wait_send()
            x_pass(t, a).wait_send()
            a_exchange(t, a).wait_send()
        q_exchange(t, 0).wait_send()
        q_exchange(t, 1).wait_send()
    @pl.when(s < SN - 1)
    def _():
        for t in range(TURNS - 1):
            for a in range(XN):
                y_copy(t, a).wait_send()

    g_sib.wait_send()
    for d in range(1, ZN):
        g_copy(d).wait_send()


def body(*args):
    vmem = pl.BlockSpec(memory_space=pltpu.VMEM)
    smem = pl.BlockSpec(memory_space=pltpu.SMEM)
    anys = pl.BlockSpec(memory_space=pl.ANY)
    dma = pltpu.SemaphoreType.DMA
    return pl.pallas_call(
        kernel,
        out_shape=(
            jax.ShapeDtypeStruct((1, TURNS, 1, B, D), BF16),
            jax.ShapeDtypeStruct((1, 24, 256), F32),
        ),
        in_specs=[anys, anys, vmem, smem, anys, anys, vmem, vmem, vmem, vmem, vmem, anys],
        out_specs=(anys, vmem),
        scratch_shapes=[
            pltpu.VMEM((TURNS, 4 * B, D), BF16),
            pltpu.VMEM((2, ZN, XN, 24, 2 * CW), BF16),
            pltpu.VMEM((D, 1024), BF16),
            pltpu.VMEM((XN, 10, 1, B), jnp.int32),
            pltpu.VMEM((XN, TURNS, B, 256), BF16),
            pltpu.VMEM((TURNS, 2, 4, 4 * B, 128), BF16),
            pltpu.VMEM((TURNS, 4, 4 * B, 128), BF16),
            pltpu.VMEM((4 * B, D), BF16),
            pltpu.VMEM((TURNS, XN, 2, B, 128), BF16),
            pltpu.VMEM((TURNS, XN, 2, B, 128), BF16),
            pltpu.VMEM((XN, 2, B, 128), BF16),
            pltpu.VMEM((TURNS, XN, B, CW), BF16),
            pltpu.VMEM((8, D), F32),
            pltpu.VMEM((512, CW), BF16),
            pltpu.VMEM((CW, 512), BF16),
            pltpu.VMEM((8, 128), F32),
            pltpu.VMEM((CW, 256), F32),
            pltpu.VMEM((192, 256), F32),
            pltpu.VMEM((192, 256), F32),
            pltpu.VMEM((ZN - 1, 24, 256), F32),
            dma((TURNS, XN, 3)),
            dma((TURNS, XN, 3)),
            dma((4,)),
            dma((TURNS - 1, XN)),
            dma((TURNS - 1, XN)),
            dma((3, 2)),
            dma((3, 2)),
            dma((2,)),
            dma((4, 2)),
            dma((4, 2)),
            dma((5, 2)),
            dma((5, 2)),
            dma((4,)),
            dma((4,)),
            dma((TURNS, 3)),
            dma((TURNS, 3)),
            dma((TURNS, 2)),
            dma((TURNS, 2)),
            dma((TURNS, XN)),
            dma((TURNS, XN)),
            dma((TURNS, XN)),
            dma((TURNS, XN)),
            dma((ZN,)),
            dma((ZN,)),
        ],
        compiler_params=pltpu.CompilerParams(
            collective_id=0, has_side_effects=True, vmem_limit_bytes=56 * 1024 * 1024
        ),
        cost_estimate=pl.CostEstimate(
            flops=10_000_000_000, bytes_accessed=16_000_000, transcendentals=7_000_000
        ),
    )(*args)


def solution(mesh):
    in_specs = (
        P("pipe", None, "dp", "seq", None),
        P(None, "dp", "seq"),
        P(None, "dp", None),
        P(None, "dp"),
        P("pipe", ("seq", "dp"), None),
        P("pipe", ("seq", "dp"), None),
        P("pipe", None),
        P("pipe", None),
        P("pipe", None, None),
        P("pipe", None),
        P("pipe", None),
        P("pipe", None, "dp", "seq", None),
    )
    out_specs = (P("pipe", None, "dp", "seq", None), P("pipe", ("seq", "dp"), None))
    return jax.shard_map(body, mesh=mesh, in_specs=in_specs, out_specs=out_specs, check_vma=False)
```

time: 504 us -> 125 us (0.25)
  waiting for transfers between devices: 362 us -> 0 us
  Pallas kernels: 0 us -> 119 us
  starting transfers between devices: 37.5 us -> 0 us
  matrix products: 35.7 us -> 0 us
  blocking collectives: 22.7 us -> 0 us
  between operations: 16.1 us -> 0.65 us
  other arithmetic: 11.6 us -> 0 us
  local copies, waits for them, and re-layouts: 12.8 us -> 4.31 us
    all_gather x2 -> x0, waiting for transfers between devices: 166 us -> none  [the longest x1 87.5 us: body(): lax.all_gather(w_query, ('seq', 'dp'), axis=1, tiled=True)]
    unnamed x4 -> x0, waiting for transfers between devices: 145 us -> none
    pallas_call x0 -> x1, Pallas kernels: none -> 119 us  [body(): pl.pallas_call(kernel, out_shape=(jax.ShapeDtypeStruct((1, TURNS, 1, B, D...]
    all_to_all x7 -> x0, waiting for transfers between devices: 36.3 us -> none  [the longest x3 20.2 us: body(): lax.all_to_all(keyval_parts, 'seq', split_axis=1, concat_axis=0, tiled=True)]
    dot_general x22 -> x0, matrix products: 35.7 us -> none  [the longest x3 9.53 us: body(): jnp.dot(normed, wquery, preferred_element_type=jnp.float32)]
    all_to_all x7 -> x0, starting transfers between devices: 30.1 us -> none  [the longest x3 13.8 us: body(): lax.all_to_all(query_parts, 'seq', split_axis=1, concat_axis=0, tiled=True)]
    all_to_all x2 -> x0, blocking collectives: 22.7 us -> none  [body(): lax.all_to_all(attended, 'seq', split_axis=0, concat_axis=1, tiled=True)]
    ppermute x2 -> x0, waiting for transfers between devices: 14.7 us -> none  [passed_along(): lax.ppermute(value, axis, [(source, source + steps) for source in range(f...]
  transfers between devices with their start and end apart: 12 -> 0, of which waited for: 11 -> 0; matrix products, arithmetic and copies ran while one was open for 5% -> 0% of each run, Pallas kernels for 0% -> 0%
where the time goes in v1:
time: 125 us; the launch traced here: 124 us
  Pallas kernels  119 us (95%)
  local copies, waits for them, and re-layouts  4.31 us (3%)
    pallas_call x1, Pallas kernels, body(): pl.pallas_call(kernel, out_shape=(jax.ShapeDtypeStruct((1, TURNS, 1, B, D...  119 us
    unnamed x5, local copies, waits for them, and re-layouts  4.31 us

profile of v1, /device:TPU:1, one launch (start us, length us, event | category | flops | bytes accessed | tf_op | source)
XLA Modules:
  0.0 124.5 jit_solution(11321417134376700640)
XLA Ops:
  0.6 1.3 %copy.14.timesteps = s32[10,1]{1,0:T(8,128)} copy(s32[10,1]{0,1:T(1,128)} %param.15) | data formatting | bytes 80 | tf_op args[3]
  2.0 119.5 %shard_map.131 = (bf16[1,3,1,128,1536]{4,3,2,1,0:T(8,128)(2,1)}, f32[1,24,256]{2,1,0:T(8,128)}) custom-call(bf16[1,3,1,128,1536]{4,3,2,1,0:T(8,128)(2,1)} %inc.1, s32[10,1,128]{2,1,0:T(1,128)} %contacts.1, s32[10,1,1024]{2,1,0:T(1,128)} %keyframes.1, s32[10,1]{1,0:T(8,128)} %copy.14.timesteps, bf16[1,24,1536]{2,1,0:T(8,128)(2,1)} %wq.1, ...), custom_call_target="tpu_custom_call" | custom-call | flops 10000000000 | bytes 16000000 | tf_op jit(solution)/shard_map/pallas_call | solution.py:467
  121.5 0.0 copy-start
  121.5 2.4 %copy.17 = bf16[1,3,1,128,1536]{4,3,2,1,0:T(8,128)(2,1)} copy(bf16[1,3,1,128,1536]{4,3,2,1,0:T(8,128)(2,1)} %get-tuple-element.4) | data formatting | bytes 2359296
  123.8 0.0 copy-done
  123.8 0.6 copy.18
Async XLA Ops:
  121.5 2.4 %copy-start = (f32[1,24,256]{2,1,0:T(8,128)S(1)}, f32[1,24,256]{2,1,0:T(8,128)}, u32[]{:S(2)}) copy-start(f32[1,24,256]{2,1,0:T(8,128)} %get-tuple-element.5) | copy-start | bytes 73732

commit v2 on v1

--- a/solution.py
+++ b/solution.py
@@ -17,6 +17,9 @@
 ZN = 8
 SN = 8
 TURNS = 3
+ORDER = (0, 1, 3, 2)
+SKEW = 3
+FORWARD_AT = (4, 7, 10, 13)
 D = 1536
 CW = 384
 HEAD = 96
@@ -38,7 +41,7 @@
 def kernel(
     inc, contacts, keyframes, timesteps, wq, wkv, gain, freq, table, kbias, gate, cot,
     out, grad,
-    xg, wr, wp, ctv, cotv, stg, rcv, act, asend, arecv, atto, ob, modv, psel, pw, qpad, gacc, grec, gsum, grz,
+    xg, wr, wp, ctv, cotv, stg, rcv, act, scales, asend, arecv, atto, ob, modv, psel, pw, qpad, gacc, grec, gsum, gpass, grz,
     xs, xrv, lx, ys, yr, ws, wrv, wl, zs, zr, bs, br, cs, cr, ks, kr, qs, qr, asm, arm, osm, orm, gs, gr,
 ):
     s = lax.axis_index("pipe")
@@ -189,7 +192,7 @@
         high = b.astype(BF16).astype(F32)
         qpad[h : h + 1, :] = jnp.where(lane == HEAD, high, 0.0) + jnp.where(lane == HEAD + 1, b - high, 0.0)
     for t in range(TURNS):
-        step = timesteps[t - s + SN - 1, 0].astype(F32)
+        step = timesteps[0, t - s + SN - 1].astype(F32)
         modv[t : t + 1, :] = gain[...] * (1.0 + 0.5 * jnp.sin(step * freq[...]))
     row = lax.broadcasted_iota(jnp.int32, (512, CW), 0)
     col = lax.broadcasted_iota(jnp.int32, (512, CW), 1)
@@ -203,70 +206,80 @@
     low = col - slot * 128
     pw[...] = jnp.where((low < HEAD) & (row == slot * HEAD + low), 1.0, 0.0).astype(BF16)
 
-    def z_blocks(k, way):
-        block = zat(-k) if way == 0 else zat(k)
-        part = wr.at[c, block] if k < ZN // 2 else wr.at[c, block, pl.ds(2 * way, 2)]
-        return part
-
-    def z_send(k, way):
-        block = zat(1 - k) if way == 0 else zat(k - 1)
-        part = wr.at[c, block] if k < ZN // 2 else wr.at[c, block, pl.ds(2 * way, 2)]
-        return remote(part, part, zs.at[k - 1, way], zr.at[k - 1, way], zdev(1 - 2 * way))
-
-    def z_arrival(k, way):
-        part = z_blocks(k, way)
-        return remote(part, part, zs.at[k - 1, way], zr.at[k - 1, way], zdev(1))
-
-    def sib_part(core, k, way):
-        block = zat(-k) if way == 0 else zat(k)
-        return wr.at[core, block] if k < ZN // 2 else wr.at[core, block, pl.ds(2 * way, 2)]
-
-    def sib_send(core, k, way):
-        part = sib_part(core, k, way)
-        return remote(part, part, bs.at[k, way], br.at[k, way], sib)
-
-    for copy in own_w:
-        copy.wait()
-    for d in (1, 3, 2):
-        for n in range(2):
-            w_arrival(d, n).wait_recv()
-    z_send(1, 0).start()
-    z_send(1, 1).start()
-    sib_send(c, 0, 0).start()
-    x_forward(0, 0)
-    x_forward(0, 1)
-
-    def z_step(k):
+    half = ZN // 2
+
+    def part(core, xx, zz, k, way):
+        block = wr.at[core, zz, xx]
+        return block if k < half else block.at[:, pl.ds(CW * way, CW)]
+
+    def came(k, way):
+        return zat(-k) if way == 0 else zat(k)
+
+    def z_send(n, k, way):
+        ref = part(c, xat(ORDER[n]), zat(1 - k) if way == 0 else zat(k - 1), k, way)
+        return remote(ref, ref, zs.at[n, k - 1, way], zr.at[n, k - 1, way], zdev(1 - 2 * way))
+
+    def z_arrival(n, k, way):
+        ref = part(c, xat(ORDER[n]), came(k, way), k, way)
+        return remote(ref, ref, zs.at[n, k - 1, way], zr.at[n, k - 1, way], zdev(1))
+
+    def sib_send(core, n, k, way):
+        ref = part(core, xat(ORDER[n]), came(k, way), k, way)
+        return remote(ref, ref, bs.at[n, k, way], br.at[n, k, way], sib)
+
+    def z_step(n, k):
+        if k == 0:
+            if n == 0:
+                for copy in own_w:
+                    copy.wait()
+            else:
+                w_arrival((XN - ORDER[n]) % XN, 0).wait_recv()
+                w_arrival((XN - ORDER[n]) % XN, 1).wait_recv()
+            z_send(n, 1, 0).start()
+            z_send(n, 1, 1).start()
+            sib_send(c, n, 0, 0).start()
+            return
         for way in range(2):
-            z_arrival(k, way).wait_recv()
-            if k < ZN // 2:
-                z_send(k + 1, way).start()
-            sib_send(c, k, way).start()
-
-    z_step(1)
-    x_forward(0, 2)
-    x_forward(0, 3)
-    for k in range(2, ZN // 2 + 1):
-        z_step(k)
+            z_arrival(n, k, way).wait_recv()
+            if k < half:
+                z_send(n, k + 1, way).start()
+            sib_send(c, n, k, way).start()
+
+    def prepare(n):
+        sib_send(1 - c, n, 0, 0).wait_recv()
+        for k in range(1, half + 1):
+            for way in range(2):
+                sib_send(1 - c, n, k, way).wait_recv()
+        xx = xat(ORDER[n])
+
+        def one(cc, _):
+            block = wr[cc, :, xx].astype(F32).reshape(ZN * 24, 2 * CW).astype(BF16)
+            dst = pl.ds(pl.multiple_of((2 * xx + cc) * 192, 64), 192)
+            wp[dst, 0:512] = dot(block[:, :CW], pw[...]).astype(BF16)
+            wp[dst, 512:1024] = dot(block[:, CW:], pw[...]).astype(BF16)
+            return 0
+
+        lax.fori_loop(0, 2, one, 0)
+
+    steps = sorted((SKEW * k + n, n, k) for n in range(XN) for k in range(half + 1))
+    ready = []
+    for at, (_, n, k) in enumerate(steps):
+        z_step(n, k)
+        if at in FORWARD_AT:
+            x_forward(0, FORWARD_AT.index(at))
+        if ready:
+            prepare(ready.pop())
+        if k == half:
+            ready.append(n)
     own_x0.wait()
+    own_cot.wait()
     for a in range(XN):
         x_finish(0, a)
+    for t in range(TURNS):
+        for d in (1, 2, 3):
+            cot_piece(t, d, x).start()
     for d in (1, 2, 3):
         ct_piece(d, xat(-d)).wait_recv()
-    sib_send(1 - c, 0, 0).wait_recv()
-    for k in range(1, ZN // 2 + 1):
-        for way in range(2):
-            sib_send(1 - c, k, way).wait_recv()
-
-    def prepare(n, _):
-        cc, xx = lax.rem(n, 2), lax.div(n, 2)
-        block = wr[cc, :, xx].astype(F32).reshape(ZN * 24, 2 * CW).astype(BF16)
-        dst = pl.ds(pl.multiple_of(n * 192, 64), 192)
-        wp[dst, 0:512] = dot(block[:, :CW], pw[...]).astype(BF16)
-        wp[dst, 512:1024] = dot(block[:, CW:], pw[...]).astype(BF16)
-        return 0
-
-    lax.fori_loop(0, 2 * XN, prepare, 0)
 
     def contact_rows(t, r):
         return ctv[r, t - s + SN - 1]
@@ -283,27 +296,22 @@
     ).astype(BF16)
     ones_lane = jnp.where(lane == HEAD, 1.0, 0.0)
 
-    def q_exchange(t, p):
-        span = pl.ds(256 * p, 256)
-        return remote(stg.at[t, 1 - c, :, span], rcv.at[t, :, span], qs.at[t, p], qr.at[t, p], sib)
-
-    def project(t, p):
-        turn = t - s + SN - 1
-        span = slice(256 * p, 256 * p + 256)
-        flags = []
-        scales = []
-        for q in range(2):
-            r = 2 * p + q
-            inner = slice(B * r, B * r + B)
-            hidden = xg[t, inner, :].astype(F32) + dot_t(onehot(contact_rows(t, r)), table[0])
-            square = jnp.sum(hidden * hidden, axis=1, keepdims=True)
-            act[inner, :] = (hidden * modv[t : t + 1, :]).astype(BF16)
-            scales.append(lax.rsqrt(square * (1.0 / D) + EPSILON))
-            flag = keyframes[turn, :, pl.ds(pl.multiple_of((2 * r + c) * B, B), B)]
-            flag = jnp.where(place == 0, flag.astype(F32), 0.0).astype(BF16)
-            flags.append(dot_t(flag, flag_lanes))
-        scale = jnp.concatenate(scales, axis=0)
-        flag = jnp.concatenate(flags, axis=0)
+    def q_exchange(t, r):
+        span = pl.ds(B * r, B)
+        return remote(stg.at[t, 1 - c, :, span], rcv.at[t, :, span], qs.at[t, r], qr.at[t, r], sib)
+
+    def norm(t, r):
+        span = slice(B * r, B * r + B)
+        hidden = xg[t, span, :].astype(F32) + dot_t(onehot(contact_rows(t, r)), table[0])
+        square = jnp.sum(hidden * hidden, axis=1, keepdims=True)
+        act[span, :] = (hidden * modv[t : t + 1, :]).astype(BF16)
+        scales[span, :] = jnp.broadcast_to(lax.rsqrt(square * (1.0 / D) + EPSILON), (B, 128))
+
+    def project(t, r):
+        span = slice(B * r, B * r + B)
+        scale = scales[span, :]
+        flag = keyframes[t - s + SN - 1, :, pl.ds(pl.multiple_of((2 * r + c) * B, B), B)]
+        flag = dot_t(jnp.where(place == 0, flag.astype(F32), 0.0).astype(BF16), flag_lanes)
         result = dot(act[span, :], wp[...])
         scale_q = scale * (LOG2E * HEAD ** (-0.5))
         for h in range(4):
@@ -314,22 +322,31 @@
             at = 512 + 256 * h
             stg[t, h, 2, span, :] = (result[:, at : at + 128] * scale + flag).astype(BF16)
             stg[t, h, 3, span, :] = (result[:, at + 128 : at + 256] * scale + ones_lane).astype(BF16)
-        q_exchange(t, p).start()
+        q_exchange(t, r).start()
+
+    for r in range(XN):
+        norm(0, r)
+    for n in ready:
+        prepare(n)
 
     def a_exchange(t, r):
         return remote(asend.at[t, r], arecv.at[t, r], asm.at[t, r], arm.at[t, r], sib)
 
     def attend(t, r):
+        keys = jnp.concatenate([stg[t, c, 2], rcv[t, 2]], axis=0)
+        values = jnp.concatenate([stg[t, c, 3], rcv[t, 3]], axis=0)
+        scores = []
         for h in range(2):
-            q = jnp.concatenate([stg[t, c, h, rows(r), :], rcv[t, h, rows(r), :]], axis=0)
-            s0 = dot_nt(q, stg[t, c, 2])
-            s1 = dot_nt(q, rcv[t, 2])
-            top = jnp.maximum(jnp.max(s0, axis=1, keepdims=True), jnp.max(s1, axis=1, keepdims=True))
-            total = dot(jnp.exp2(s0 - top).astype(BF16), stg[t, c, 3])
-            total = total + dot(jnp.exp2(s1 - top).astype(BF16), rcv[t, 3])
+            scores.append(dot_nt(stg[t, c, h, rows(r), :], keys))
+            scores.append(dot_nt(rcv[t, h, rows(r), :], keys))
+        powers = [jnp.exp2(each - jnp.max(each, axis=1, keepdims=True)).astype(BF16) for each in scores]
+        for n, each in enumerate(powers):
+            total = dot(each, values)
             result = (total * (1.0 / total[:, HEAD : HEAD + 1])).astype(BF16)
-            atto[r, h] = result[:B]
-            asend[t, r, h] = result[B:]
+            if n % 2 == 0:
+                atto[r, n // 2] = result
+            else:
+                asend[t, r, n // 2] = result
         a_exchange(t, r).start()
 
     def finish(t, r):
@@ -359,49 +376,62 @@
         return pltpu.make_async_copy(ob.at[t, x], out.at[0, t, 0, :, cols(x)], osm.at[t, 0])
 
     for t in range(TURNS):
-        if t > 0:
+        if t == 0:
+            for r in range(XN):
+                project(t, r)
+        else:
+            x_start(t, 2)
             x_forward(t, 0)
+            x_start(t, 3)
             x_forward(t, 1)
-            x_start(t, 2)
-            x_start(t, 3)
             x_forward(t, 2)
             x_forward(t, 3)
             for a in range(XN):
-                x_finish(t, a)
-        project(t, 0)
-        project(t, 1)
-        if t == 0:
-            own_cot.wait()
-        for d in (1, 2, 3):
-            cot_piece(t, d, x).start()
-        if t > 0:
+                if a == 0:
+                    x_finish(t, 0)
+
+                    @pl.when(s == 0)
+                    def _(t=t):
+                        for later in range(1, XN):
+                            x_finish(t, later)
+                else:
+                    @pl.when(s > 0)
+                    def _(t=t, a=a):
+                        x_finish(t, a)
+
+                norm(t, a)
+                project(t, a)
             out_own(t - 1).start()
-            for d in (1, 2, 3):
+            for d in (2, 1, 3):
                 out_copy(t - 1, d).start()
-        q_exchange(t, 0).wait_recv()
-        q_exchange(t, 1).wait_recv()
-
-        def step(r, _, t=t):
-            attend(t, r)
-
-            @pl.when(r > 0)
+        for r in range(XN):
+            q_exchange(t, r).wait_recv()
+
+        def step(n, _, t=t):
+            attend(t, n if t + 1 < TURNS else xat(n + 1))
+
+            @pl.when(n > 0)
             def _():
-                finish(t, r - 1)
+                if t + 1 < TURNS:
+                    finish(t, n - 1)
+                else:
+                    finish(t, xat(n))
+                    out_copy(t, n).start()
 
             return 0
 
         lax.fori_loop(0, XN, step, 0)
         if t + 1 < TURNS:
             x_start(t + 1, 0)
-        finish(t, XN - 1)
-        if t + 1 < TURNS:
+            finish(t, XN - 1)
             x_start(t + 1, 1)
         else:
+            finish(t, x)
             out_own(t).start()
-            for d in (1, 2, 3):
-                out_copy(t, d).start()
-        for d in (1, 2, 3):
-            cot_piece(t, d, xat(-d)).wait_recv()
+        if t == 0:
+            for n in range(TURNS):
+                for d in (1, 2, 3):
+                    cot_piece(n, d, xat(-d)).wait_recv()
         share = dot_t(ob[t].reshape(XN * B, CW), cotv[:, t].reshape(XN * B, 256))
         gacc[...] = share if t == 0 else gacc[...] + share
 
@@ -411,10 +441,11 @@
     g_sib.start()
     g_sib.wait_recv()
     gsum[...] = gacc[pl.ds(pl.multiple_of(c * 192, 64), 192), :] + grec[...]
+    gpass[...] = gsum[...].reshape(ZN, 24, 256).astype(BF16)
 
     def g_copy(d):
         return remote(
-            gsum.at[pl.ds(pl.multiple_of(24 * zat(d), 8), 24)], grz.at[d - 1], gs.at[d], gr.at[d], zdev(d)
+            gpass.at[zat(d)], grz.at[d - 1], gs.at[d], gr.at[d], zdev(d)
         )
 
     for d in (4, 3, 5, 2, 6, 1, 7):
@@ -422,19 +453,20 @@
     total = gsum[pl.ds(pl.multiple_of(24 * j, 8), 24), :]
     for d in (1, 7, 2, 6, 3, 5, 4):
         g_copy(d).wait_recv()
-        total = total + grz[d - 1]
+        total = total + grz[d - 1].astype(F32)
     grad[0] = total * (float(TURNS * ZN * 1024) ** (-0.5))
 
     for d in (1, 2, 3):
         for n, w in enumerate((wq, wkv)):
             w_piece(d, n, w).wait_send()
         ct_piece(d, x).wait_send()
-    for k in range(ZN // 2 + 1):
-        for way in range(2):
-            if k > 0:
-                z_send(k, way).wait_send()
-            if k > 0 or way == 0:
-                sib_send(c, k, way).wait_send()
+    for n in range(XN):
+        for k in range(half + 1):
+            for way in range(2):
+                if k > 0:
+                    z_send(n, k, way).wait_send()
+                if k > 0 or way == 0:
+                    sib_send(c, n, k, way).wait_send()
     for t in range(TURNS):
         out_own(t).wait()
         for d in (1, 2, 3):
@@ -446,8 +478,7 @@
             x_send(t, a, 1).wait_send()
             x_pass(t, a).wait_send()
             a_exchange(t, a).wait_send()
-        q_exchange(t, 0).wait_send()
-        q_exchange(t, 1).wait_send()
+            q_exchange(t, a).wait_send()
     @pl.when(s < SN - 1)
     def _():
         for t in range(TURNS - 1):
@@ -460,6 +491,8 @@
 
 
 def body(*args):
+    args = list(args)
+    args[3] = args[3].reshape(1, args[3].shape[0])
     vmem = pl.BlockSpec(memory_space=pltpu.VMEM)
     smem = pl.BlockSpec(memory_space=pltpu.SMEM)
     anys = pl.BlockSpec(memory_space=pl.ANY)
@@ -467,11 +500,11 @@
     return pl.pallas_call(
         kernel,
         out_shape=(
-            jax.ShapeDtypeStruct((1, TURNS, 1, B, D), BF16),
-            jax.ShapeDtypeStruct((1, 24, 256), F32),
+            pltpu.VMEM((1, TURNS, 1, B, D), BF16),
+            pltpu.VMEM((1, 24, 256), F32),
         ),
         in_specs=[anys, anys, vmem, smem, anys, anys, vmem, vmem, vmem, vmem, vmem, anys],
-        out_specs=(anys, vmem),
+        out_specs=(vmem, vmem),
         scratch_shapes=[
             pltpu.VMEM((TURNS, 4 * B, D), BF16),
             pltpu.VMEM((2, ZN, XN, 24, 2 * CW), BF16),
@@ -481,6 +514,7 @@
             pltpu.VMEM((TURNS, 2, 4, 4 * B, 128), BF16),
             pltpu.VMEM((TURNS, 4, 4 * B, 128), BF16),
             pltpu.VMEM((4 * B, D), BF16),
+            pltpu.VMEM((4 * B, 128), F32),
             pltpu.VMEM((TURNS, XN, 2, B, 128), BF16),
             pltpu.VMEM((TURNS, XN, 2, B, 128), BF16),
             pltpu.VMEM((XN, 2, B, 128), BF16),
@@ -492,7 +526,8 @@
             pltpu.VMEM((CW, 256), F32),
             pltpu.VMEM((192, 256), F32),
             pltpu.VMEM((192, 256), F32),
-            pltpu.VMEM((ZN - 1, 24, 256), F32),
+            pltpu.VMEM((ZN, 24, 256), BF16),
+            pltpu.VMEM((ZN - 1, 24, 256), BF16),
             dma((TURNS, XN, 3)),
             dma((TURNS, XN, 3)),
             dma((4,)),
@@ -501,16 +536,16 @@
             dma((3, 2)),
             dma((3, 2)),
             dma((2,)),
-            dma((4, 2)),
-            dma((4, 2)),
-            dma((5, 2)),
-            dma((5, 2)),
+            dma((XN, 4, 2)),
+            dma((XN, 4, 2)),
+            dma((XN, 5, 2)),
+            dma((XN, 5, 2)),
             dma((4,)),
             dma((4,)),
             dma((TURNS, 3)),
             dma((TURNS, 3)),
-            dma((TURNS, 2)),
-            dma((TURNS, 2)),
+            dma((TURNS, XN)),
+            dma((TURNS, XN)),
             dma((TURNS, XN)),
             dma((TURNS, XN)),
             dma((TURNS, XN)),

time: 125 us -> 105 us (0.84)
  Pallas kernels: 119 us -> 103 us
  local copies, waits for them, and re-layouts: 4.31 us -> 1.62 us
    pallas_call x1, Pallas kernels: 119 us -> 103 us  [body(): pl.pallas_call(kernel, out_shape=(pltpu.VMEM((1, TURNS, 1, B, D), BF16),...]
    unnamed x5 -> x2, local copies, waits for them, and re-layouts: 4.31 us -> 1.62 us
where the time goes in v2:
time: 105 us
  Pallas kernels  103 us (98%)
  local copies, waits for them, and re-layouts  1.62 us (2%)
    pallas_call x1, Pallas kernels, body(): pl.pallas_call(kernel, out_shape=(pltpu.VMEM((1, TURNS, 1, B, D), BF16),...  103 us

profile of v2, /device:TPU:1, one launch (start us, length us, event | category | flops | bytes accessed | tf_op | source)
XLA Modules:
  0.0 105.3 jit_solution(8434962789090423041)
XLA Ops:
  0.6 103.0 %shard_map.131 = (bf16[1,3,1,128,1536]{4,3,2,1,0:T(8,128)(2,1)S(1)}, f32[1,24,256]{2,1,0:T(8,128)S(1)}) custom-call(bf16[1,3,1,128,1536]{4,3,2,1,0:T(8,128)(2,1)} %inc.1, s32[10,1,128]{2,1,0:T(1,128)} %contacts.1, s32[10,1,1024]{2,1,0:T(1,128)} %keyframes.1, s32[1,10]{1,0:T(1,128)} %bitcast.1, bf16[1,24,1536]{2,1,0:T(8,128)(2,1)} %wq.1, ...), custom_call_target="tpu_custom_call" | custom-call | flops 10000000000 | bytes 16000000 | tf_op jit(solution)/shard_map/pallas_call | solution.py:500
  103.7 1.0 copy.16
  104.7 0.6 copy.17

commit v3 on v2

--- a/solution.py
+++ b/solution.py
@@ -407,20 +407,14 @@
         for r in range(XN):
             q_exchange(t, r).wait_recv()
 
-        def step(n, _, t=t):
+        for n in range(XN):
             attend(t, n if t + 1 < TURNS else xat(n + 1))
-
-            @pl.when(n > 0)
-            def _():
+            if n > 0:
                 if t + 1 < TURNS:
                     finish(t, n - 1)
                 else:
                     finish(t, xat(n))
                     out_copy(t, n).start()
-
-            return 0
-
-        lax.fori_loop(0, XN, step, 0)
         if t + 1 < TURNS:
             x_start(t + 1, 0)
             finish(t, XN - 1)

time: 105 us -> 106 us (level)
  no operation moved by 1% of the time
where the time goes in v3:
time: 106 us; the launch traced here: 105 us
  Pallas kernels  103 us (97%)
  local copies, waits for them, and re-layouts  1.62 us (2%)
    pallas_call x1, Pallas kernels, body(): pl.pallas_call(kernel, out_shape=(pltpu.VMEM((1, TURNS, 1, B, D), BF16),...  103 us

profile of v3, /device:TPU:1, one launch (start us, length us, event | category | flops | bytes accessed | tf_op | source)
XLA Modules:
  0.0 105.4 jit_solution(3120470406910355328)
XLA Ops:
  0.6 103.1 %shard_map.131 = (bf16[1,3,1,128,1536]{4,3,2,1,0:T(8,128)(2,1)S(1)}, f32[1,24,256]{2,1,0:T(8,128)S(1)}) custom-call(bf16[1,3,1,128,1536]{4,3,2,1,0:T(8,128)(2,1)} %inc.1, s32[10,1,128]{2,1,0:T(1,128)} %contacts.1, s32[10,1,1024]{2,1,0:T(1,128)} %keyframes.1, s32[1,10]{1,0:T(1,128)} %bitcast.1, bf16[1,24,1536]{2,1,0:T(8,128)(2,1)} %wq.1, ...), custom_call_target="tpu_custom_call" | custom-call | flops 10000000000 | bytes 16000000 | tf_op jit(solution)/shard_map/pallas_call | solution.py:494
  103.8 1.0 copy.16
  104.8 0.6 copy.17
